TPU v7x, 32 devices: a whole 2x2x4 slice. The times are simulated.
32 devices in a mesh: energy: 8 (over z, y), momentum: 4 (over x, core).
Axes of the slice: x: 2, y: 2, z: 4, core: 2. Of those that a mesh axis runs over, the one named last changes fastest.
Arguments:
- lesser: bfloat16 [8, 4, 2, 512, 512], P('energy', 'momentum'), may hold values from -6 to 6
- greater: bfloat16 [8, 4, 2, 512, 512], P('energy', 'momentum'), may hold values from -6 to 6
- retarded: bfloat16 [8, 4, 2, 512, 512], P('energy', 'momentum'), may hold values from -4.1875 to 4.1875
- occupation: float32 [2], replicated, may hold values from 0.1 to 2
- shift_slots: int32 [2, 2, 8], replicated, may hold values from 0 to 8, as said below
- coupling: int32 [2, 4, 4], replicated, may hold values from 1 to 8
Outputs:
- lesser_new: bfloat16 [8, 4, 2, 512, 512], P('energy', 'momentum')
- greater_new: bfloat16 [8, 4, 2, 512, 512], P('energy', 'momentum')
- retarded_new: bfloat16 [8, 4, 2, 512, 512], P('energy', 'momentum')
Inputs may be any that keep to these rules, and one draw needn't show every extreme that they name: The energies of the grid are held in slots in an order of their own, one energy a slot. Mode m has one shift, the same for all slots: shift_slots[m, 0, j] is the slot of the energy that lies that shift below the energy of slot j, shift_slots[m, 1, j] the slot of the energy as far above it, and 8 where that energy lies outside the grid.
All inputs are finite; a program needn't handle non-finite values.
Results may differ from a plain program's by a relative error of at most 0.0064.
Values may be sent and summed in bfloat16 or wider, within the bound.
A program may use at most 64 MiB of HBM per device.

v0:
```python
import jax
import jax.numpy as jnp
from jax import lax
from jax.sharding import PartitionSpec as P


def matrix_product(former, latter):
    return jnp.matmul(former, latter, preferred_element_type=jnp.float32)


def complex_product(former, latter):
    former_re = former[..., 0, :, :]
    former_im = former[..., 1, :, :]
    latter_re = latter[..., 0, :, :]
    latter_im = latter[..., 1, :, :]
    real_part = matrix_product(former_re, latter_re) - matrix_product(former_im, latter_im)
    imag_part = matrix_product(former_re, latter_im) + matrix_product(former_im, latter_re)
    return jnp.stack([real_part, imag_part], axis=-3)


def adjoint_product(former, propagator):
    former_re = former[..., 0, :, :]
    former_im = former[..., 1, :, :]
    prop_re = jnp.swapaxes(propagator[..., 0, :, :], -1, -2)
    prop_im = jnp.swapaxes(propagator[..., 1, :, :], -1, -2)
    real_part = matrix_product(former_re, prop_re) + matrix_product(former_im, prop_im)
    imag_part = matrix_product(former_im, prop_re) - matrix_product(former_re, prop_im)
    return jnp.stack([real_part, imag_part], axis=-3)


def scattering(less_part, more_part, weights, occupation, shift_slots):
    slots = less_part.shape[0]
    slot_ids = jnp.arange(slots, dtype=jnp.int32)
    picked = (shift_slots[..., None] == slot_ids).astype(jnp.float32)
    phonons = occupation[:, None, None]
    pick_less = phonons * picked[:, 0] + (phonons + 1.0) * picked[:, 1]
    pick_more = (phonons + 1.0) * picked[:, 0] + phonons * picked[:, 1]
    mixer_less = jnp.einsum("mjs,mkq->jksq", pick_less, weights, precision=lax.Precision.HIGHEST)
    mixer_more = jnp.einsum("mjs,mkq->jksq", pick_more, weights, precision=lax.Precision.HIGHEST)
    total_less = jnp.einsum(
        "jksq,sqxab->jkxab",
        mixer_less,
        less_part.astype(jnp.float32),
        precision=lax.Precision.HIGHEST,
    )
    total_more = jnp.einsum(
        "jksq,sqxab->jkxab",
        mixer_more,
        more_part.astype(jnp.float32),
        precision=lax.Precision.HIGHEST,
    )
    return (total_less, total_more)


def per_device(lesser, greater, retarded, occupation, shift_slots, coupling):
    momenta = coupling.shape[1]
    modes = coupling.shape[0]
    order = lesser.shape[3]
    factor = 1.0 / (order * 4.0 * (modes * momenta) ** 0.5)
    weights = coupling.astype(jnp.float32)
    rows_less, rows_more = (
        lax.all_to_all(lesser, "energy", split_axis=3, concat_axis=0, tiled=True),
        lax.all_to_all(greater, "energy", split_axis=3, concat_axis=0, tiled=True),
    )
    own_index = lax.axis_index("momentum")
    pieces = (
        lax.all_gather(rows_less, "momentum", axis=1, tiled=True),
        lax.all_gather(rows_more, "momentum", axis=1, tiled=True),
    )
    count = pieces[0].shape[1]
    chosen = lax.dynamic_slice(weights, (0, own_index, 0), (modes, 1, count))
    add_less, add_more = scattering(pieces[0], pieces[1], chosen, occupation, shift_slots)
    sigma_less = (add_less * factor).astype(jnp.bfloat16)
    sigma_more = (add_more * factor).astype(jnp.bfloat16)
    sigma_less, sigma_more = (
        lax.all_to_all(sigma_less, "energy", split_axis=0, concat_axis=3, tiled=True),
        lax.all_to_all(sigma_more, "energy", split_axis=0, concat_axis=3, tiled=True),
    )
    sigma_ret = ((sigma_more.astype(jnp.float32) - sigma_less.astype(jnp.float32)) * 0.5).astype(
        jnp.bfloat16
    )
    stacked = jnp.stack([sigma_less, sigma_more, sigma_ret])
    halfway = complex_product(retarded[None], stacked).astype(jnp.bfloat16)
    lesser_new = adjoint_product(halfway[0], retarded).astype(jnp.bfloat16)
    greater_new = adjoint_product(halfway[1], retarded).astype(jnp.bfloat16)
    retarded_new = (retarded.astype(jnp.float32) + complex_product(halfway[2], retarded)).astype(
        jnp.bfloat16
    )
    return (lesser_new, greater_new, retarded_new)


def solution(mesh):
    return jax.shard_map(
        per_device,
        mesh=mesh,
        in_specs=(
            P("energy", "momentum", None, None, None),
            P("energy", "momentum", None, None, None),
            P("energy", "momentum", None, None, None),
            P(),
            P(),
            P(),
        ),
        out_specs=(
            P("energy", "momentum", None, None, None),
            P("energy", "momentum", None, None, None),
            P("energy", "momentum", None, None, None),
        ),
        check_vma=False,
    )
```

profile of v0, /device:TPU:0, one launch (start us, length us, event | category | flops | bytes accessed | tf_op | source)
XLA Modules:
  0.0 179.2 jit_solution(12115761878033358903)
XLA Ops:
  7.2 0.0 all-gather.5.cloned.1.call-start
  7.2 2.3 %copy.29 = bf16[1,1,2,512,512]{4,2,1,0,3:T(2,128)(2,1)S(1)} copy(bf16[1,1,2,512,512]{4,3,2,1,0:T(8,128)(2,1)} %param.6) | data formatting | bytes 2097152 | tf_op args[0]
  9.5 33.0 %all_to_all.66 = bf16[1,1,2,512,512]{4,2,1,0,3:T(2,128)(2,1)S(1)} all-to-all(bf16[1,1,2,512,512]{4,2,1,0,3:T(2,128)(2,1)S(1)} %copy.29), channel_id=1, replica_groups=mesh['energy'=8,'momentum'=4] {'energy'}, dimensions={3} | all-to-all | bytes 2097152 | tf_op jit(solution)/shard_map/all_to_all | solution.py:62
  42.5 1.5 copy.69
  44.1 0.0 all-gather.7.cloned.1.call-start
  44.1 1.1 copy.36
  45.3 28.8 %all_to_all.67 = bf16[1,1,2,512,512]{4,2,1,0,3:T(2,128)(2,1)S(1)} all-to-all(bf16[1,1,2,512,512]{4,2,1,0,3:T(2,128)(2,1)S(1)} %copy.36), channel_id=1, replica_groups=mesh['energy'=8,'momentum'=4] {'energy'}, dimensions={3} | all-to-all | bytes 2097152 | tf_op jit(solution)/shard_map/all_to_all | solution.py:63
  74.1 1.5 copy.68
  75.7 0.7 dynamic-slice_convert_fusion
  76.4 0.1 fusion.68
  76.5 0.1 add_bitcast_fusion
  76.6 0.2 convolution_bitcast_fusion.1
  76.8 1.0 all-gather.5.cloned.1.call-done
  77.8 9.7 %fusion.15 = bf16[8,1,2,64,512]{4,0,3,2,1:T(8,128)(2,1)S(1)} fusion(bf16[8,4,1,2,64,512]{5,0,1,4,3,2:T(8,128)(2,1)} %all-gather.5.cloned.1.call-done, f32[8,8,4,1,1]{1,2,0,4,3:T(4,128)S(1)} %convolution_bitcast_fusion.1), kind=kOutput, calls=%fused_computation.24 | convolution fusion | flops 202375168 | bytes 5243904 | tf_op jit(solution)/shard_map/jksq,sqxab->jkxab/dot_general | solution.py:40
  87.4 1.3 copy.33
  88.7 5.5 %all-to-all-start.1 = ((bf16[8,1,2,64,512]{4,3,2,1,0:T(8,128)(2,1)}), bf16[8,1,2,64,512]{4,3,2,1,0:T(8,128)(2,1)S(1)}, u32[]{:S(2)}, u32[]{:S(2)}) async-start(bf16[8,1,2,64,512]{4,3,2,1,0:T(8,128)(2,1)} %copy.33), calls=%async_computation.1 | async-start | bytes 2097152 | tf_op jit(solution)/shard_map/all_to_all | solution.py:76
  94.2 0.2 convolution_bitcast_fusion
  94.4 20.0 %all-gather.7.cloned.1.call-done = bf16[8,4,1,2,64,512]{5,0,1,4,3,2:T(8,128)(2,1)} async-done(((bf16[8,1,1,2,64,512]{5,0,1,4,3,2:T(8,128)(2,1)}), bf16[8,4,1,2,64,512]{5,0,1,4,3,2:T(8,128)(2,1)}) %all-gather.7.cloned.1.call-update) | async-done | bytes 4194320 | tf_op jit(solution)/shard_map/all_gather | solution.py:68
  114.4 9.7 %fusion.18 = bf16[8,1,2,64,512]{4,0,3,2,1:T(8,128)(2,1)S(1)} fusion(bf16[8,4,1,2,64,512]{5,0,1,4,3,2:T(8,128)(2,1)} %all-gather.7.cloned.1.call-done, f32[8,8,4,1,1]{1,2,0,4,3:T(4,128)S(1)} %convolution_bitcast_fusion), kind=kOutput, calls=%fused_computation.25 | convolution fusion | flops 202375168 | bytes 5243904 | tf_op jit(solution)/shard_map/jksq,sqxab->jkxab/dot_general | solution.py:46
  124.0 1.3 copy.40
  125.3 5.5 %all-to-all-start.3 = ((bf16[8,1,2,64,512]{4,3,2,1,0:T(8,128)(2,1)}), bf16[8,1,2,64,512]{4,3,2,1,0:T(8,128)(2,1)S(1)}, u32[]{:S(2)}, u32[]{:S(2)}) async-start(bf16[8,1,2,64,512]{4,3,2,1,0:T(8,128)(2,1)} %copy.40), calls=%async_computation.3 | async-start | bytes 2097152 | tf_op jit(solution)/shard_map/all_to_all | solution.py:77
  130.8 0.1 copy.34
  130.9 0.5 copy.44
  131.5 25.5 %all-to-all-done.3 = bf16[8,1,2,64,512]{4,3,2,1,0:T(8,128)(2,1)S(1)} async-done(((bf16[8,1,2,64,512]{4,3,2,1,0:T(8,128)(2,1)}), bf16[8,1,2,64,512]{4,3,2,1,0:T(8,128)(2,1)S(1)}, u32[]{:S(2)}, u32[]{:S(2)}) %all-to-all-start.3) | async-done | bytes 1048608 | tf_op jit(solution)/shard_map/all_to_all | solution.py:77
  157.0 0.1 copy.41
  157.1 0.5 copy.45
  157.7 0.3 multiply_convert_fusion
  158.0 0.3 pad_maximum_fusion
  158.4 0.9 copy-done
  159.2 1.0 fusion.14
  160.2 1.0 fusion.13
  161.3 1.1 fusion.12
  162.3 1.1 fusion.11
  163.4 0.3 fusion.35
  163.7 0.5 fusion.36
  164.1 0.5 fusion.40
  164.6 0.5 fusion.50
  165.1 0.5 fusion.52
  165.6 0.5 fusion.46
  166.1 0.5 fusion.48
  166.6 0.5 fusion.21
  167.0 0.5 fusion.22
  167.5 0.5 fusion.29
  168.0 0.5 fusion.30
  168.5 0.5 fusion.27
  169.0 0.5 fusion.28
  169.5 1.4 fusion.4
  170.8 1.5 pad_maximum_fusion.2
  (12 shorter events, 0.1 us)
Async XLA Ops:
  7.2 70.6 %all-gather.5.cloned.1.call-start = ((), (), s32[]{:S(2)}) async-start(), calls=%async_computation.4 | async-start | bytes 5242880 | tf_op jit(solution)/shard_map/all_gather | solution.py:67
  9.5 34.6 %copy-start.1 = (bf16[1,1,2,512,512]{4,3,2,1,0:T(8,128)(2,1)S(1)}, bf16[1,1,2,512,512]{4,3,2,1,0:T(8,128)(2,1)}, u32[]{:S(2)}) copy-start(bf16[1,1,2,512,512]{4,3,2,1,0:T(8,128)(2,1)} %param.7) | copy-start | bytes 3145732
  44.1 70.3 %all-gather.7.cloned.1.call-start = ((), (), s32[]{:S(2)}) async-start(), calls=%async_computation.5 | async-start | bytes 5242880 | tf_op jit(solution)/shard_map/all_gather | solution.py:68
  45.2 30.5 %copy-start.2 = (s32[2,2,8]{2,1,0:T(2,128)S(1)}, s32[2,2,8]{2,1,0:T(2,128)}, u32[]{:S(2)}) copy-start(s32[2,2,8]{2,1,0:T(2,128)} %param.10) | copy-start | bytes 388
  45.2 31.2 %copy-start.3 = (f32[2]{0:T(128)S(1)}, f32[2]{0:T(128)}, u32[]{:S(2)}) copy-start(f32[2]{0:T(128)} %param.9) | copy-start | bytes 28
  88.7 36.6 %all-to-all-start.1 = ((bf16[8,1,2,64,512]{4,3,2,1,0:T(8,128)(2,1)}), bf16[8,1,2,64,512]{4,3,2,1,0:T(8,128)(2,1)S(1)}, u32[]{:S(2)}, u32[]{:S(2)}) async-start(bf16[8,1,2,64,512]{4,3,2,1,0:T(8,128)(2,1)} %copy.33), calls=%async_computation.1 | async-start | bytes 2097152 | tf_op jit(solution)/shard_map/all_to_all | solution.py:76
  125.3 31.7 %all-to-all-start.3 = ((bf16[8,1,2,64,512]{4,3,2,1,0:T(8,128)(2,1)}), bf16[8,1,2,64,512]{4,3,2,1,0:T(8,128)(2,1)S(1)}, u32[]{:S(2)}, u32[]{:S(2)}) async-start(bf16[8,1,2,64,512]{4,3,2,1,0:T(8,128)(2,1)} %copy.40), calls=%async_computation.3 | async-start | bytes 2097152 | tf_op jit(solution)/shard_map/all_to_all | solution.py:77
  158.0 1.2 copy-start
Sparse Core Ops, SparseCore 0:
  44.2 33.5 all-gather.4
  79.9 34.4 all-gather.6
where the time goes:
time: 180 us; the launch traced here: 179 us
  blocking collectives  61.8 us (34%)
  waiting for transfers between devices  46.5 us (26%)
  matrix products  29.6 us (16%)
  between operations  14.3 us (8%)
  local copies, waits for them, and re-layouts  11.2 us (6%)
  starting transfers between devices  11.1 us (6%)
  other arithmetic  4.65 us (3%)
    all_to_all x1, blocking collectives, per_device(): lax.all_to_all(lesser, 'energy', split_axis=3, concat_axis=0, tiled=True)  33 us
    all_to_all x1, blocking collectives, per_device(): lax.all_to_all(greater, 'energy', split_axis=3, concat_axis=0, tiled=True)  28.8 us
    all_to_all x1, waiting for transfers between devices, per_device(): lax.all_to_all(sigma_more, 'energy', split_axis=0, concat_axis=3, tiled=T...  25.5 us
    all_gather x1, waiting for transfers between devices, per_device(): lax.all_gather(rows_more, 'momentum', axis=1, tiled=True)  20 us
    dot_general x16, matrix products, matrix_product(): return jnp.matmul(former, latter, preferred_element_type=jnp.float32)  9.88 us
    dot_general x1, matrix products, scattering(): jnp.einsum('jksq,sqxab->jkxab', mixer_less, less_part.astype(jnp.float32)...  9.66 us
    dot_general x1, matrix products, scattering(): jnp.einsum('jksq,sqxab->jkxab', mixer_more, more_part.astype(jnp.float32)...  9.66 us
    all_to_all x1, starting transfers between devices, per_device(): lax.all_to_all(sigma_more, 'energy', split_axis=0, concat_axis=3, tiled=T...  5.52 us
  transfers between devices with their start and end apart: 4, of which 3 were waited for; matrix products, arithmetic and copies ran while one was open for 15% of the time, Pallas kernels for 0%

commit v1 on v0

--- a/solution.py
+++ b/solution.py
@@ -1,7 +1,36 @@
+import functools
 import jax
 import jax.numpy as jnp
 from jax import lax
 from jax.sharding import PartitionSpec as P
+
+
+def measure_lanes(arr, on_dim, matrix):
+    x_next, newest = (arr.shape[:on_dim], arr.shape[on_dim + 1 :])
+    return jnp.moveaxis(arr.reshape(*x_next, matrix, -1, *newest), on_dim, 0)
+
+
+def map_paths(frame_in, dim_i):
+    frame_in = jnp.moveaxis(frame_in, 0, dim_i)
+    piece_next = frame_in.shape
+    return frame_in.reshape(
+        *piece_next[:dim_i], piece_next[dim_i] * piece_next[dim_i + 1], *piece_next[dim_i + 2 :]
+    )
+
+
+def connect_masks_here(sheet, comm_axis, panel, own_rows):
+    f_now, view_out = (lax.axis_size(comm_axis), lax.axis_index(comm_axis))
+    z = measure_lanes(sheet, panel, f_now)
+    t1 = z
+    for ix in range(1, f_now):
+        item_now, clean = ((view_out + ix) % f_now, (view_out - ix) % f_now)
+        z_new = lax.dynamic_index_in_dim(z, item_now, 0)
+        a_next = lax.ppermute(z_new, comm_axis, [(q, (q + ix) % f_now) for q in range(f_now)])
+        t1 = lax.dynamic_update_slice_in_dim(t1, a_next, clean, axis=0)
+    return map_paths(t1, own_rows)
+
+
+replace_node_on = functools.partial(connect_masks_here, comm_axis="energy", panel=0, own_rows=3)
 
 
 def matrix_product(former, latter):
@@ -74,7 +103,7 @@
     sigma_more = (add_more * factor).astype(jnp.bfloat16)
     sigma_less, sigma_more = (
         lax.all_to_all(sigma_less, "energy", split_axis=0, concat_axis=3, tiled=True),
-        lax.all_to_all(sigma_more, "energy", split_axis=0, concat_axis=3, tiled=True),
+        replace_node_on(sigma_more),
     )
     sigma_ret = ((sigma_more.astype(jnp.float32) - sigma_less.astype(jnp.float32)) * 0.5).astype(
         jnp.bfloat16

time: 180 us -> 209 us (1.16)
  the two profiles are of different devices: /device:TPU:0 before, /device:TPU:20 now
where the time goes in v1:
time: 209 us; the launch traced here: 208 us
  blocking collectives  57.5 us (28%)
  starting transfers between devices  34.1 us (16%)
  local copies, waits for them, and re-layouts  34 us (16%)
  waiting for transfers between devices  33.9 us (16%)
  matrix products  29.6 us (14%)
  between operations  14.4 us (7%)
  other arithmetic  4.65 us (2%)
    all_to_all x1, blocking collectives, per_device(): lax.all_to_all(greater, 'energy', split_axis=3, concat_axis=0, tiled=True)  29.1 us
    all_to_all x1, blocking collectives, per_device(): lax.all_to_all(lesser, 'energy', split_axis=3, concat_axis=0, tiled=True)  28.4 us
    ppermute x7, starting transfers between devices, connect_masks_here(): lax.ppermute(z_new, comm_axis, [(q, (q + ix) % f_now) for q in range(f_no...  28 us
    dynamic_update_slice x7, local copies, waits for them, and re-layouts, connect_masks_here(): t1 = lax.dynamic_update_slice_in_dim(t1, a_next, clean, axis=0)  20.7 us
    all_gather x1, waiting for transfers between devices, per_device(): lax.all_gather(rows_more, 'momentum', axis=1, tiled=True)  19.5 us
    ppermute x7, waiting for transfers between devices, connect_masks_here(): lax.ppermute(z_new, comm_axis, [(q, (q + ix) % f_now) for q in range(f_no...  10.8 us
    dot_general x16, matrix products, matrix_product(): return jnp.matmul(former, latter, preferred_element_type=jnp.float32)  9.88 us
    dot_general x1, matrix products, scattering(): jnp.einsum('jksq,sqxab->jkxab', mixer_less, less_part.astype(jnp.float32)...  9.66 us
  transfers between devices with their start and end apart: 10, of which 4 were waited for; matrix products, arithmetic and copies ran while one was open for 24% of the time, Pallas kernels for 0%

profile of v1, /device:TPU:20, one launch (start us, length us, event | category | flops | bytes accessed | tf_op | source)
XLA Modules:
  0.0 208.1 jit_solution(15639654489243674358)
XLA Ops:
  7.2 2.3 %copy.29 = bf16[1,1,2,512,512]{4,2,1,0,3:T(2,128)(2,1)S(1)} copy(bf16[1,1,2,512,512]{4,3,2,1,0:T(8,128)(2,1)} %param.6) | data formatting | bytes 2097152 | tf_op args[0]
  9.5 28.4 %all_to_all.51 = bf16[1,1,2,512,512]{4,2,1,0,3:T(2,128)(2,1)S(1)} all-to-all(bf16[1,1,2,512,512]{4,2,1,0,3:T(2,128)(2,1)S(1)} %copy.29), channel_id=1, replica_groups=mesh['energy'=8,'momentum'=4] {'energy'}, dimensions={3} | all-to-all | bytes 2097152 | tf_op jit(solution)/shard_map/all_to_all | solution.py:91
  38.0 1.5 copy.68
  39.6 1.1 copy.36
  40.7 29.1 %all_to_all.52 = bf16[1,1,2,512,512]{4,2,1,0,3:T(2,128)(2,1)S(1)} all-to-all(bf16[1,1,2,512,512]{4,2,1,0,3:T(2,128)(2,1)S(1)} %copy.36), channel_id=1, replica_groups=mesh['energy'=8,'momentum'=4] {'energy'}, dimensions={3} | all-to-all | bytes 2097152 | tf_op jit(solution)/shard_map/all_to_all | solution.py:92
  69.8 1.5 copy.67
  71.4 0.7 fusion.68
  72.5 3.6 %all-gather.5.cloned.1.call-done = bf16[8,4,1,2,64,512]{5,0,1,4,3,2:T(8,128)(2,1)} async-done(((bf16[8,1,1,2,64,512]{5,0,1,4,3,2:T(8,128)(2,1)}), bf16[8,4,1,2,64,512]{5,0,1,4,3,2:T(8,128)(2,1)}) %all-gather.5.cloned.1.call-update) | async-done | bytes 4194320 | tf_op jit(solution)/shard_map/all_gather | solution.py:96
  76.0 9.7 %fusion.15 = bf16[8,1,2,64,512]{4,0,3,2,1:T(8,128)(2,1)S(1)} fusion(bf16[8,4,1,2,64,512]{5,0,1,4,3,2:T(8,128)(2,1)} %all-gather.5.cloned.1.call-done, f32[8,8,4,1,1]{1,2,0,4,3:T(4,128)S(1)} %convolution_bitcast_fusion.1), kind=kOutput, calls=%fused_computation.24 | convolution fusion | flops 202375168 | bytes 5243904 | tf_op jit(solution)/shard_map/jksq,sqxab->jkxab/dot_general | solution.py:69
  85.7 1.3 copy.33
  87.0 6.0 %all-to-all-start.1 = ((bf16[8,1,2,64,512]{4,3,2,1,0:T(8,128)(2,1)}), bf16[8,1,2,64,512]{4,3,2,1,0:T(8,128)(2,1)S(1)}, u32[]{:S(2)}, u32[]{:S(2)}) async-start(bf16[8,1,2,64,512]{4,3,2,1,0:T(8,128)(2,1)} %copy.33), calls=%async_computation.1 | async-start | bytes 2097152 | tf_op jit(solution)/shard_map/all_to_all | solution.py:105
  93.2 19.5 %all-gather.7.cloned.1.call-done = bf16[8,4,1,2,64,512]{5,0,1,4,3,2:T(8,128)(2,1)} async-done(((bf16[8,1,1,2,64,512]{5,0,1,4,3,2:T(8,128)(2,1)}), bf16[8,4,1,2,64,512]{5,0,1,4,3,2:T(8,128)(2,1)}) %all-gather.7.cloned.1.call-update) | async-done | bytes 4194320 | tf_op jit(solution)/shard_map/all_gather | solution.py:97
  112.7 9.7 %fusion.5 = bf16[8,2,64,512]{3,0,2,1:T(8,128)(2,1)S(1)} fusion(bf16[8,4,1,2,64,512]{5,0,1,4,3,2:T(8,128)(2,1)} %all-gather.7.cloned.1.call-done, f32[8,8,4,1,1]{1,2,0,4,3:T(4,128)S(1)} %convolution_bitcast_fusion), kind=kOutput, calls=%fused_computation.14 | convolution fusion | flops 202375168 | bytes 5243904 | tf_op jit(solution)/shard_map/jksq,sqxab->jkxab/dot_general | solution.py:75
  122.4 2.9 %dynamic-slice_bitcast_fusion = (bf16[1,1,1,2,64,512]{5,0,4,3,2,1:T(2,128)(2,1)}, bf16[1,1,1,2,64,512]{5,0,4,3,2,1:T(2,128)(2,1)}, bf16[1,1,1,2,64,512]{5,0,4,3,...) fusion(bf16[8,2,64,512]{3,0,2,1:T(8,128)(2,1)S(1)} %fusion.5, ...), kind=kLoop, calls=%fused_computation.79 | loop fusion | bytes 1835036 | tf_op jit(solution)/shard_map/jit(dynamic_index_in_dim)/dynamic_slice | solution.py:27
  125.2 1.5 collective-permute-start.1
  126.7 0.5 collective-permute-start
  127.2 1.5 collective-permute-start.4
  128.7 2.3 %collective-permute-start.2 = (bf16[1,1,1,2,64,512]{5,0,4,3,2,1:T(2,128)(2,1)}, bf16[1,1,1,2,64,512]{5,0,4,3,2,1:T(2,128)(2,1)}, u32[]{:S(2)}, u32[]{:S(2)}) collective-permute-start(bf16[1,1,1,2,64,512]{5,0,4,3,2,1:T(2,128)(2,1)} %get-tuple-element.10), channel_id=1, source_target_pairs={{0,12},{4,16},{8,20},{12,24},{16,28},{20,0},{24,4},{28,8},{1,13},{... | collective-permute-start | bytes 393224 | tf_op jit(solution)/shard_map/ppermute | solution.py:28
  131.0 1.5 collective-permute-start.3
  132.5 1.8 collective-permute-done.1
  134.4 0.5 collective-permute-start.5
  134.9 9.0 %collective-permute-done = bf16[1,1,1,2,64,512]{5,0,4,3,2,1:T(2,128)(2,1)} collective-permute-done((bf16[1,1,1,2,64,512]{5,0,4,3,2,1:T(2,128)(2,1)S(1)}, bf16[1,1,1,2,64,512]{5,0,4,3,2,1:T(2,128)(2,1)}, u32[]{:S(2)}, u32[]{:S(2)}) %collective-permute-start) | collective-permute-done | bytes 131104 | tf_op jit(solution)/shard_map/ppermute | solution.py:28
  143.9 20.1 %collective-permute-start.6 = (bf16[1,1,1,2,64,512]{5,0,4,3,2,1:T(2,128)(2,1)}, bf16[1,1,1,2,64,512]{5,0,4,3,2,1:T(2,128)(2,1)S(1)}, u32[]{:S(2)}, u32[]{:S(2)}) collective-permute-start(bf16[1,1,1,2,64,512]{5,0,4,3,2,1:T(2,128)(2,1)} %get-tuple-element.6), channel_id=1, source_target_pairs={{0,28},{4,0},{8,4},{12,8},{16,12},{20,16},{24,20},{28,24},{1,29},{... | collective-permute-start | bytes 393224 | tf_op jit(solution)/shard_map/ppermute | solution.py:28
  164.0 4.4 %dynamic_update_slice.21 = bf16[8,1,1,2,64,512]{5,0,4,3,2,1:T(8,128)(2,1)S(1)} dynamic-update-slice(bf16[8,1,1,2,64,512]{5,0,4,3,2,1:T(8,128)(2,1)S(1)} %bitcast.191, bf16[1,1,1,2,64,512]{5,0,4,3,2,1:T(2,128)(2,1)} %collective-permute-done, s32[]{:T(128)S(6)} %select_n.109, s32[]{:T(128)} %constant.102.clone.1, s32[]{:T(128)} %constant.102.clone.1, s32[]{:T(128)} %constant.102.clone.1, ...) | dynamic-update-slice | bytes 262148 | tf_op jit(solution)/shard_map/dynamic_update_slice | solution.py:29
  168.5 2.4 %dynamic_update_slice.22 = bf16[8,1,1,2,64,512]{5,0,4,3,2,1:T(8,128)(2,1)S(1)} dynamic-update-slice(bf16[8,1,1,2,64,512]{5,0,4,3,2,1:T(8,128)(2,1)S(1)} %dynamic_update_slice.21, bf16[1,1,1,2,64,512]{5,0,4,3,2,1:T(2,128)(2,1)S(1)} %collective-permute-done.1, s32[]{:T(128)S(6)} %select_n.113, s32[]{:T(128)} %constant.102.clone.1, s32[]{:T(128)} %constant.102.clone.1, s32[]{:T(128)} %constant.102.clone.1, ...) | dynamic-update-slice | bytes 262148 | tf_op jit(solution)/shard_map/dynamic_update_slice | solution.py:29
  170.9 4.5 %dynamic_update_slice.23 = bf16[8,1,1,2,64,512]{5,0,4,3,2,1:T(8,128)(2,1)S(1)} dynamic-update-slice(bf16[8,1,1,2,64,512]{5,0,4,3,2,1:T(8,128)(2,1)S(1)} %dynamic_update_slice.22, bf16[1,1,1,2,64,512]{5,0,4,3,2,1:T(2,128)(2,1)} %collective-permute-done.2, s32[]{:T(128)S(6)} %select_n.117, s32[]{:T(128)} %constant.102.clone.1, s32[]{:T(128)} %constant.102.clone.1, s32[]{:T(128)} %constant.102.clone.1, ...) | dynamic-update-slice | bytes 262148 | tf_op jit(solution)/shard_map/dynamic_update_slice | solution.py:29
  175.3 2.4 %dynamic_update_slice.24 = bf16[8,1,1,2,64,512]{5,0,4,3,2,1:T(8,128)(2,1)S(1)} dynamic-update-slice(bf16[8,1,1,2,64,512]{5,0,4,3,2,1:T(8,128)(2,1)S(1)} %dynamic_update_slice.23, bf16[1,1,1,2,64,512]{5,0,4,3,2,1:T(2,128)(2,1)S(1)} %collective-permute-done.3, s32[]{:T(128)S(6)} %select_n.121, s32[]{:T(128)} %constant.102.clone.1, s32[]{:T(128)} %constant.102.clone.1, s32[]{:T(128)} %constant.102.clone.1, ...) | dynamic-update-slice | bytes 262148 | tf_op jit(solution)/shard_map/dynamic_update_slice | solution.py:29
  177.7 2.4 %dynamic_update_slice.25 = bf16[8,1,1,2,64,512]{5,0,4,3,2,1:T(8,128)(2,1)S(1)} dynamic-update-slice(bf16[8,1,1,2,64,512]{5,0,4,3,2,1:T(8,128)(2,1)S(1)} %dynamic_update_slice.24, bf16[1,1,1,2,64,512]{5,0,4,3,2,1:T(2,128)(2,1)S(1)} %collective-permute-done.4, s32[]{:T(128)S(6)} %select_n.125, s32[]{:T(128)} %constant.102.clone.1, s32[]{:T(128)} %constant.102.clone.1, s32[]{:T(128)} %constant.102.clone.1, ...) | dynamic-update-slice | bytes 262148 | tf_op jit(solution)/shard_map/dynamic_update_slice | solution.py:29
  180.1 2.4 %dynamic_update_slice.26 = bf16[8,1,1,2,64,512]{5,0,4,3,2,1:T(8,128)(2,1)S(1)} dynamic-update-slice(bf16[8,1,1,2,64,512]{5,0,4,3,2,1:T(8,128)(2,1)S(1)} %dynamic_update_slice.25, bf16[1,1,1,2,64,512]{5,0,4,3,2,1:T(2,128)(2,1)S(1)} %collective-permute-done.5, s32[]{:T(128)S(6)} %select_n.129, s32[]{:T(128)} %constant.102.clone.1, s32[]{:T(128)} %constant.102.clone.1, s32[]{:T(128)} %constant.102.clone.1, ...) | dynamic-update-slice | bytes 262148 | tf_op jit(solution)/shard_map/dynamic_update_slice | solution.py:29
  182.5 2.4 %dynamic_update_slice.27 = bf16[8,1,1,2,64,512]{5,0,4,3,2,1:T(8,128)(2,1)S(1)} dynamic-update-slice(bf16[8,1,1,2,64,512]{5,0,4,3,2,1:T(8,128)(2,1)S(1)} %dynamic_update_slice.26, bf16[1,1,1,2,64,512]{5,0,4,3,2,1:T(2,128)(2,1)S(1)} %collective-permute-done.6, s32[]{:T(128)S(6)} %select_n.133, s32[]{:T(128)} %constant.102.clone.1, s32[]{:T(128)} %constant.102.clone.1, s32[]{:T(128)} %constant.102.clone.1, ...) | dynamic-update-slice | bytes 262148 | tf_op jit(solution)/shard_map/dynamic_update_slice | solution.py:29
  185.2 0.5 copy.44
  185.8 0.8 copy.43
  187.3 0.9 copy-done
  188.2 1.0 fusion.14
  189.2 1.0 fusion.13
  190.2 1.1 fusion.12
  191.3 1.1 fusion.11
  193.1 0.5 fusion.37
  193.5 0.5 fusion.47
  194.0 0.5 fusion.49
  194.5 0.5 fusion.43
  195.0 0.5 fusion.45
  196.4 0.5 fusion.26
  196.9 0.5 fusion.27
  197.4 0.5 fusion.24
  197.9 0.5 fusion.25
  198.4 1.4 fusion.4
  199.8 1.5 pad_maximum_fusion.2
  (31 shorter events, 3.5 us)
Async XLA Ops:
  7.2 68.9 %all-gather.5.cloned.1.call-start = ((), (), s32[]{:S(2)}) async-start(), calls=%async_computation.3 | async-start | bytes 5242880 | tf_op jit(solution)/shard_map/all_gather | solution.py:96
  9.5 30.1 %copy-start.1 = (bf16[1,1,2,512,512]{4,3,2,1,0:T(8,128)(2,1)S(1)}, bf16[1,1,2,512,512]{4,3,2,1,0:T(8,128)(2,1)}, u32[]{:S(2)}) copy-start(bf16[1,1,2,512,512]{4,3,2,1,0:T(8,128)(2,1)} %param.7) | copy-start | bytes 3145732
  39.5 73.2 %all-gather.7.cloned.1.call-start = ((), (), s32[]{:S(2)}) async-start(), calls=%async_computation.4 | async-start | bytes 5242880 | tf_op jit(solution)/shard_map/all_gather | solution.py:97
  40.7 30.7 %copy-start.2 = (s32[2,2,8]{2,1,0:T(2,128)S(1)}, s32[2,2,8]{2,1,0:T(2,128)}, u32[]{:S(2)}) copy-start(s32[2,2,8]{2,1,0:T(2,128)} %param.10) | copy-start | bytes 388
  40.7 31.4 %copy-start.3 = (f32[2]{0:T(128)S(1)}, f32[2]{0:T(128)}, u32[]{:S(2)}) copy-start(f32[2]{0:T(128)} %param.9) | copy-start | bytes 28
  87.0 98.7 %all-to-all-start.1 = ((bf16[8,1,2,64,512]{4,3,2,1,0:T(8,128)(2,1)}), bf16[8,1,2,64,512]{4,3,2,1,0:T(8,128)(2,1)S(1)}, u32[]{:S(2)}, u32[]{:S(2)}) async-start(bf16[8,1,2,64,512]{4,3,2,1,0:T(8,128)(2,1)} %copy.33), calls=%async_computation.1 | async-start | bytes 2097152 | tf_op jit(solution)/shard_map/all_to_all | solution.py:105
  125.2 9.1 %collective-permute-start.1 = (bf16[1,1,1,2,64,512]{5,0,4,3,2,1:T(2,128)(2,1)S(1)}, bf16[1,1,1,2,64,512]{5,0,4,3,2,1:T(2,128)(2,1)S(1)}, u32[]{:S(2)}, u32[]{:S(2)}) collective-permute-start(bf16[1,1,1,2,64,512]{5,0,4,3,2,1:T(2,128)(2,1)S(1)} %get-tuple-element.11), channel_id=1, source_target_pairs={{0,8},{4,12},{8,16},{12,20},{16,24},{20,28},{24,0},{28,4},{1,9},{5... | collective-permute-start | bytes 393224 | tf_op jit(solution)/shard_map/ppermute | solution.py:28
  126.7 17.2 %collective-permute-start = (bf16[1,1,1,2,64,512]{5,0,4,3,2,1:T(2,128)(2,1)S(1)}, bf16[1,1,1,2,64,512]{5,0,4,3,2,1:T(2,128)(2,1)}, u32[]{:S(2)}, u32[]{:S(2)}) collective-permute-start(bf16[1,1,1,2,64,512]{5,0,4,3,2,1:T(2,128)(2,1)S(1)} %get-tuple-element.12), channel_id=1, source_target_pairs={{0,4},{4,8},{8,12},{12,16},{16,20},{20,24},{24,28},{28,0},{1,5},{5... | collective-permute-start | bytes 393224 | tf_op jit(solution)/shard_map/ppermute | solution.py:28
  127.2 50.5 %collective-permute-start.4 = (bf16[1,1,1,2,64,512]{5,0,4,3,2,1:T(2,128)(2,1)}, bf16[1,1,1,2,64,512]{5,0,4,3,2,1:T(2,128)(2,1)S(1)}, u32[]{:S(2)}, u32[]{:S(2)}) collective-permute-start(bf16[1,1,1,2,64,512]{5,0,4,3,2,1:T(2,128)(2,1)} %get-tuple-element.8), channel_id=1, source_target_pairs={{0,20},{4,24},{8,28},{12,0},{16,4},{20,8},{24,12},{28,16},{1,21},{... | collective-permute-start | bytes 393224 | tf_op jit(solution)/shard_map/ppermute | solution.py:28
  128.7 42.1 %collective-permute-start.2 = (bf16[1,1,1,2,64,512]{5,0,4,3,2,1:T(2,128)(2,1)}, bf16[1,1,1,2,64,512]{5,0,4,3,2,1:T(2,128)(2,1)}, u32[]{:S(2)}, u32[]{:S(2)}) collective-permute-start(bf16[1,1,1,2,64,512]{5,0,4,3,2,1:T(2,128)(2,1)} %get-tuple-element.10), channel_id=1, source_target_pairs={{0,12},{4,16},{8,20},{12,24},{16,28},{20,0},{24,4},{28,8},{1,13},{... | collective-permute-start | bytes 393224 | tf_op jit(solution)/shard_map/ppermute | solution.py:28
  131.0 44.3 %collective-permute-start.3 = (bf16[1,1,1,2,64,512]{5,0,4,3,2,1:T(2,128)(2,1)}, bf16[1,1,1,2,64,512]{5,0,4,3,2,1:T(2,128)(2,1)S(1)}, u32[]{:S(2)}, u32[]{:S(2)}) collective-permute-start(bf16[1,1,1,2,64,512]{5,0,4,3,2,1:T(2,128)(2,1)} %get-tuple-element.9), channel_id=1, source_target_pairs={{0,16},{4,20},{8,24},{12,28},{16,0},{20,4},{24,8},{28,12},{1,17},{... | collective-permute-start | bytes 393224 | tf_op jit(solution)/shard_map/ppermute | solution.py:28
  134.4 45.7 %collective-permute-start.5 = (bf16[1,1,1,2,64,512]{5,0,4,3,2,1:T(2,128)(2,1)}, bf16[1,1,1,2,64,512]{5,0,4,3,2,1:T(2,128)(2,1)S(1)}, u32[]{:S(2)}, u32[]{:S(2)}) collective-permute-start(bf16[1,1,1,2,64,512]{5,0,4,3,2,1:T(2,128)(2,1)} %get-tuple-element.7), channel_id=1, source_target_pairs={{0,24},{4,28},{8,0},{12,4},{16,8},{20,12},{24,16},{28,20},{1,25},{... | collective-permute-start | bytes 393224 | tf_op jit(solution)/shard_map/ppermute | solution.py:28
  143.9 38.6 %collective-permute-start.6 = (bf16[1,1,1,2,64,512]{5,0,4,3,2,1:T(2,128)(2,1)}, bf16[1,1,1,2,64,512]{5,0,4,3,2,1:T(2,128)(2,1)S(1)}, u32[]{:S(2)}, u32[]{:S(2)}) collective-permute-start(bf16[1,1,1,2,64,512]{5,0,4,3,2,1:T(2,128)(2,1)} %get-tuple-element.6), channel_id=1, source_target_pairs={{0,28},{4,0},{8,4},{12,8},{16,12},{20,16},{24,20},{28,24},{1,29},{... | collective-permute-start | bytes 393224 | tf_op jit(solution)/shard_map/ppermute | solution.py:28
  186.9 1.2 copy-start
Sparse Core Ops, SparseCore 0:
  39.7 36.3 all-gather.4
  78.2 34.4 all-gather.6
